TPU v7x, 128 devices: a whole 4x4x4 slice. The times are simulated.
128 devices in a mesh: col: 8 (over z, core), row: 16 (over x, y).
Axes of the slice: x: 4, y: 4, z: 4, core: 2. Of those that a mesh axis runs over, the one named last changes fastest.
Arguments:
- affinity: bfloat16 [15360, 128, 128], P(('col', 'row')), may hold values from 0 to 0.015625
- tile_rows: int32 [15360], P(('col', 'row')), may hold values from 0 to 39
- tile_cols: int32 [15360], P(('col', 'row')), may hold values from 0 to 79
- live_tiles: int32 [128], P(('col', 'row')), may hold values from 1 to 120, as said below
- start: float32 [81920, 256], P(('col', 'row')), may hold values from -1500 to 1500
Outputs:
- vectors: float32 [81920, 256], P(('col', 'row'))
- first_passes: float32 [2, 81920, 256], P(None, ('col', 'row'))
Inputs may be any that keep to these rules, and one draw needn't show every extreme that they name: A device's tiles are its slots 0 to live_tiles - 1; later slots are ignored. Some device holds exactly 120 tiles.
All inputs are finite; a program needn't handle non-finite values.
Results may differ from a plain program's by a relative error of at most 0.0003.
Values sent between devices are 32-bit elements; how exact they have to be, the bound alone decides.
A program may use at most 128 MiB of HBM per device.

v0:
```python
import jax
import jax.numpy as jnp
from jax import lax
from jax.sharding import Mesh
from jax.sharding import PartitionSpec as P

ITERS = 2
ROW = ("row_0", "row_1")
COL = ("col_0", "col_1")
COL_ROW = ("col_0", "col_1", "row_0", "row_1")


highest = lax.Precision.HIGHEST


def cut_along(value, dim, devices):
    before, after = (value.shape[:dim], value.shape[dim + 1 :])
    return jnp.moveaxis(value.reshape(*before, devices, -1, *after), dim, 0)


def sent_and_summed(value, axis, dim):
    parts = cut_along(value, dim, lax.axis_size(axis))
    arrived = lax.all_to_all(parts, axis, split_axis=0, concat_axis=0, tiled=True)
    return arrived.sum(axis=0)


def sum_in_two_steps(value, axes, dim):
    far, near = axes
    parts = cut_along(value, dim, lax.axis_size(far))
    nearer = sent_and_summed(parts, near, dim + 1)
    arrived = lax.all_to_all(nearer, far, split_axis=0, concat_axis=0, tiled=True)
    return arrived.sum(axis=0)


def rows_for(lines, devices):
    spare = -lines.shape[0] % devices
    if not spare:
        return lines
    return jnp.concatenate([lines, jnp.zeros((spare, *lines.shape[1:]), lines.dtype)])


def sent_to_all(value, axis):
    copies = jnp.broadcast_to(value, (lax.axis_size(axis), *value.shape))
    return lax.all_to_all(copies, axis, split_axis=0, concat_axis=0, tiled=True)


def joined_along(parts, dim):
    lengths = list(parts.shape[1:])
    lengths[dim] *= parts.shape[0]
    return jnp.moveaxis(parts, 0, dim).reshape(lengths)


def whole_of(value, axes, dim):
    far, near = axes
    initial = sent_to_all(value, far)
    parts = jnp.swapaxes(sent_to_all(initial, near), 0, 1)
    return joined_along(parts.reshape(-1, *value.shape), dim)


def nested_sum(value, axes):
    lines = value.reshape(-1, value.shape[-1])
    own = sum_in_two_steps(
        rows_for(lines, lax.axis_size(axes[0]) * lax.axis_size(axes[1])), axes, 0
    )
    whole = whole_of(own, axes, 0)
    return whole[: len(lines)].reshape(value.shape)


def total_of(value, axes):
    own = sum_in_two_steps(
        rows_for(value, lax.axis_size(axes[0]) * lax.axis_size(axes[1])), axes, 0
    )
    whole = whole_of(own, axes, 0)
    return whole[: len(value)].reshape(value.shape)


def together(arrays, axis):
    ends = [0]
    for a in arrays:
        ends.append(ends[-1] + a.size)
    subtotal = total_of(jnp.concatenate([a.ravel() for a in arrays]), axis)
    return tuple((subtotal[b:e].reshape(a.shape) for a, b, e in zip(arrays, ends, ends[1:])))


def local_gram(matrix):
    return jnp.dot(matrix.T, matrix, precision=highest, preferred_element_type=jnp.float32)


def inverse_lower(gram):
    lower = jnp.linalg.cholesky(gram)
    return jax.scipy.linalg.solve_triangular(
        lower, jnp.eye(gram.shape[0], dtype=jnp.float32), lower=True
    )


def apply_factor(matrix, inverse):
    return jnp.dot(matrix, inverse.T, precision=highest, preferred_element_type=jnp.float32)


def body(affinity, tile_rows, tile_cols, live_tiles, start):
    n_row = lax.axis_size(ROW)
    n_col = lax.axis_size(COL)
    slot_count = affinity.shape[0]
    tile_size = affinity.shape[1]
    rows_local = start.shape[0]
    vec_count = start.shape[1]
    own_tiles = rows_local // tile_size
    live = (jnp.arange(slot_count) < live_tiles[0]).astype(jnp.float32)
    row_onehot = (jnp.arange(own_tiles * n_col)[:, None] == tile_rows[None, :]).astype(
        jnp.float32
    ) * live[None, :]
    row_sums = jnp.sum(affinity, axis=2, dtype=jnp.float32)
    degree_terms = jnp.dot(
        row_onehot, row_sums, precision=highest, preferred_element_type=jnp.float32
    )
    degree = 1.0 + sent_and_summed(degree_terms, COL, 0).reshape(rows_local)
    scaling = (1.0 / jnp.sqrt(degree))[:, None]
    squares = affinity.astype(jnp.float32)
    firsts = []
    pending = start
    for step_number in range(ITERS):
        mapped_scaled = scaling * pending
        gathered = lax.all_gather(mapped_scaled, ROW, axis=0, tiled=True)
        gathered = gathered.reshape(n_row * own_tiles, tile_size, vec_count)
        picked = gathered[tile_cols]
        products = jnp.einsum(
            "sij,sjk->sik", squares, picked, precision=highest, preferred_element_type=jnp.float32
        )
        terms = jnp.dot(
            row_onehot,
            products.reshape(slot_count, tile_size * vec_count),
            precision=highest,
            preferred_element_type=jnp.float32,
        )
        summed = sum_in_two_steps(terms, ("col_0", "col_1"), 0)
        raw_image = scaling * (mapped_scaled + summed.reshape(rows_local, vec_count))
        if step_number == 0:
            inner_gram = nested_sum(local_gram(raw_image), (("col_0", "col_1", "row_0"), "row_1"))
            image_block = raw_image
        else:
            raw_gram, pending_gram = together(
                (local_gram(raw_image), local_gram(pending)), (("col_0", "col_1", "row_0"), "row_1")
            )
            pending_inverse = inverse_lower(pending_gram)
            image_block = apply_factor(raw_image, pending_inverse)
            inner_gram = jnp.dot(
                jnp.dot(
                    pending_inverse, raw_gram, precision=highest, preferred_element_type=jnp.float32
                ),
                pending_inverse.T,
                precision=highest,
                preferred_element_type=jnp.float32,
            )
        pending = apply_factor(image_block, inverse_lower(inner_gram))
        firsts.append(pending)
    final_gram = nested_sum(local_gram(pending), (("col_0", "col_1", "row_0"), "row_1"))
    basis = apply_factor(pending, inverse_lower(final_gram))
    total_images = rows_local * n_row * n_col
    root = jnp.sqrt(jnp.float32(total_images))
    return (root * basis, root * jnp.stack(firsts, axis=0))


def solution(mesh):
    torus = Mesh(mesh.devices.reshape(4, 2, 4, 4), ("col_0", "col_1", "row_0", "row_1"))
    return jax.shard_map(
        body,
        mesh=torus,
        in_specs=(P(COL_ROW, None, None), P(COL_ROW), P(COL_ROW), P(COL_ROW), P(COL_ROW, None)),
        out_specs=(P(COL_ROW, None), P(None, COL_ROW, None)),
        check_vma=False,
    )
```

profile of v0, /device:TPU:0, one launch (start us, length us, event | category | flops | bytes accessed | tf_op | source)
XLA Modules:
  0.0 914.5 jit_solution(9744506423480880370)
XLA Ops:
  12.6 5.4 all-to-all-start
  18.1 5.4 all-to-all-done
  26.3 79.2 %all-gather.3.cloned.1.call-done = f32[10240,256]{1,0:T(8,128)} async-done(((f32[640,256]{1,0:T(8,128)}), f32[10240,256]{1,0:T(8,128)}) %all-gather.3.cloned.1.call-update) | async-done | bytes 10485776 | tf_op jit(solution)/shard_map/all_gather | solution.py:123
  105.5 13.6 %gather_fusion = f32[120,128,256]{2,1,0:T(8,128)} fusion(f32[80,128,256]{2,1,0:T(8,128)} %bitcast.176, s32[1024]{0:T(1024)S(1)} %pad_clamp_fusion), kind=kCustom, calls=%fused_computation | custom fusion | bytes 31457760 | tf_op jit(solution)/shard_map/gather | solution.py:125
  119.1 20.2 %convolution_bitcast_fusion.3 = f32[120,128,256]{1,2,0:T(8,128)} fusion(f32[120,128,256]{2,1,0:T(8,128)} %gather_fusion, bf16[120,128,128]{2,1,0:T(8,128)(2,1)} %param.8), kind=kOutput, calls=%fused_computation.15 | convolution fusion | flops 6039797760 | bytes 35389440 | tf_op jit(solution)/shard_map/sij,sjk->sik/dot_general | solution.py:126
  139.3 15.6 %copy.101 = f32[120,128,256]{2,1,0:T(8,128)} copy(f32[120,128,256]{1,2,0:T(8,128)} %convolution_bitcast_fusion.3) | data formatting | bytes 31457280 | tf_op jit(solution)/shard_map/sij,sjk->sik/dot_general | solution.py:126
  154.9 17.9 %reshape.193 = f32[120,32768,1,1]{1,0,2,3:T(8,128)} reshape(f32[120,128,256]{2,1,0:T(8,128)} %copy.101) | data formatting | bytes 31457280 | tf_op jit(solution)/shard_map/reshape | solution.py:131
  172.8 16.1 %convolution_bitcast_fusion.1 = f32[2,4,5,32768]{3,2,0,1:T(8,128)S(1)} fusion(f32[120,32768,1,1]{1,0,2,3:T(8,128)} %reshape.193, f32[120]{0:T(128)S(1)} %compare_convert_fusion, s32[120]{0:T(128)S(1)} %copy-done.1, s32[4,2,5]{2,1,0:T(2,128)S(1)} %multiply_add_fusion), kind=kOutput, calls=%fused_computation.11 | convolution fusion | flops 1887446400 | bytes 20972640 | tf_op jit(solution)/shard_map/dot_general | solution.py:129
  192.3 9.1 all_to_all.93
  207.5 63.5 %all_to_all.97 = f32[4,5,32768]{2,1,0:T(8,128)} all-to-all(f32[4,5,32768]{2,1,0:T(8,128)S(1)} %copy.103), channel_id=1, replica_groups=mesh['col_0'=4,'col_1'=2,'row_0'=4,'row_1'=4] {'col_0'}, dimensions={0} | all-to-all | bytes 5242880 | tf_op jit(solution)/shard_map/all_to_all | solution.py:31
  275.5 10.7 %all_to_all.98 = f32[4,32,2,256]{3,2,1,0:T(2,128)S(1)} all-to-all(f32[4,32,2,256]{3,2,1,0:T(2,128)S(1)} %bitcast.182), channel_id=1, replica_groups=mesh['col_0'=4,'col_1'=2,'row_0'=4,'row_1'=4] {'row_1'}, dimensions={0} | all-to-all | bytes 524288 | tf_op jit(solution)/shard_map/all_to_all | solution.py:23
  286.3 11.0 %all_to_all.99 = f32[32,2,256]{2,1,0:T(2,128)S(1)} all-to-all(f32[32,2,256]{2,1,0:T(2,128)S(1)} %reduce_sum.112), channel_id=1, replica_groups=mesh['col_0'=4,'col_1'=2,'row_0'=4,'row_1'=4] {'col_0','col_1','row_0'}, dimensions={0} | all-to-all | bytes 131072 | tf_op jit(solution)/shard_map/all_to_all | solution.py:31
  301.9 7.4 all-to-all-done.5
  313.6 7.1 all-to-all-done.6
  321.1 11.7 %cholesky.214 = f32[128,128]{1,0:T(8,128)S(1)} custom-call(f32[128,128]{1,0:T(8,128)S(1)} %cholesky.346), custom_call_target="Cholesky" | custom-call | tf_op jit(solution)/shard_map/jit(cholesky)/cholesky | solution.py:90
  332.9 9.8 %custom-call.17 = f32[1,128,128]{1,2,0:T(8,128)S(1)} custom-call(f32[1,128,128]{2,1,0:T(8,128)S(1)} %get-tuple-element.91), custom_call_target="InvertDiagBlocksLowerTriangular" | custom-call | tf_op jit(solution)/shard_map/jit(cholesky)/cholesky | solution.py:90
  343.2 11.7 %cholesky.231 = f32[128,128]{1,0:T(8,128)S(1)} custom-call(f32[128,128]{1,0:T(8,128)S(1)} %convolution_subtract_fusion.7), custom_call_target="Cholesky" | custom-call | tf_op jit(solution)/shard_map/jit(cholesky)/cholesky | solution.py:90
  357.1 4.5 while.8
  362.2 19.7 %custom-call.18 = f32[2,128,128]{1,2,0:T(8,128)S(1)} custom-call(f32[2,128,128]{2,1,0:T(8,128)S(1)} %get-tuple-element.30), custom_call_target="InvertDiagBlocksLowerTriangular" | custom-call | tf_op jit(solution)/shard_map/jit(_solve_triangular)/triangular_solve | solution.py:91
  384.4 75.9 %all-gather.5.cloned.1.call-done = f32[10240,256]{1,0:T(8,128)} async-done(((f32[640,256]{1,0:T(8,128)}), f32[10240,256]{1,0:T(8,128)}) %all-gather.5.cloned.1.call-update) | async-done | bytes 10485776 | tf_op jit(solution)/shard_map/all_gather | solution.py:123
  460.3 13.6 %gather_fusion.1 = f32[120,128,256]{2,1,0:T(8,128)} fusion(f32[80,128,256]{2,1,0:T(8,128)} %bitcast.177, s32[1024]{0:T(1024)S(1)} %pad_clamp_fusion), kind=kCustom, calls=%fused_computation.1 | custom fusion | bytes 31457760 | tf_op jit(solution)/shard_map/gather | solution.py:125
  473.9 20.2 %convolution_bitcast_fusion.2 = f32[120,128,256]{1,2,0:T(8,128)} fusion(f32[120,128,256]{2,1,0:T(8,128)} %gather_fusion.1, bf16[120,128,128]{2,1,0:T(8,128)(2,1)} %param.8), kind=kOutput, calls=%fused_computation.14 | convolution fusion | flops 6039797760 | bytes 35389440 | tf_op jit(solution)/shard_map/sij,sjk->sik/dot_general | solution.py:126
  494.1 15.6 %copy.109 = f32[120,128,256]{2,1,0:T(8,128)} copy(f32[120,128,256]{1,2,0:T(8,128)} %convolution_bitcast_fusion.2) | data formatting | bytes 31457280 | tf_op jit(solution)/shard_map/sij,sjk->sik/dot_general | solution.py:126
  509.7 17.9 %reshape.194 = f32[120,32768,1,1]{1,0,2,3:T(8,128)} reshape(f32[120,128,256]{2,1,0:T(8,128)} %copy.109) | data formatting | bytes 31457280 | tf_op jit(solution)/shard_map/reshape | solution.py:131
  527.5 16.0 %convolution_bitcast_fusion = f32[2,4,5,32768]{3,2,0,1:T(8,128)S(1)} fusion(f32[120,32768,1,1]{1,0,2,3:T(8,128)} %reshape.194, f32[120]{0:T(128)S(1)} %copy-done.3, s32[120]{0:T(128)S(1)} %copy-done.1, s32[4,2,5]{2,1,0:T(2,128)S(1)} %multiply_add_fusion), kind=kOutput, calls=%fused_computation.10 | convolution fusion | flops 1887446400 | bytes 20972640 | tf_op jit(solution)/shard_map/dot_general | solution.py:129
  547.0 9.1 all_to_all.94
  564.1 4.9 all-to-all-start.8
  570.5 47.9 %all-to-all-done.8 = f32[4,5,32768]{2,1,0:T(8,128)} async-done(((f32[4,5,32768]{2,1,0:T(8,128)}), f32[4,5,32768]{2,1,0:T(8,128)}, u32[]{:S(2)}, u32[]{:S(2)}) %all-to-all-start.8) | async-done | bytes 2621472 | tf_op jit(solution)/shard_map/all_to_all | solution.py:31
  623.1 13.0 %all_to_all.100 = f32[4,32,1024]{2,1,0:T(8,128)S(1)} all-to-all(f32[4,32,1024]{2,1,0:T(8,128)S(1)} %maximum_bitcast_fusion), channel_id=1, replica_groups=mesh['col_0'=4,'col_1'=2,'row_0'=4,'row_1'=4] {'row_1'}, dimensions={0} | all-to-all | bytes 1048576 | tf_op jit(solution)/shard_map/all_to_all | solution.py:23
  636.2 11.8 %all_to_all.101 = f32[32,1,1024]{2,1,0:T(1,128)S(1)} all-to-all(f32[32,1,1024]{2,1,0:T(1,128)S(1)} %all_to_all.67), channel_id=1, replica_groups=mesh['col_0'=4,'col_1'=2,'row_0'=4,'row_1'=4] {'col_0','col_1','row_0'}, dimensions={0} | all-to-all | bytes 262144 | tf_op jit(solution)/shard_map/all_to_all | solution.py:31
  648.1 11.5 %all_to_all.95 = f32[32,1,1024]{2,1,0:T(1,128)S(1)} all-to-all(f32[32,1,1024]{2,1,0:T(1,128)S(1)} %broadcast_in_dim.30), channel_id=1, replica_groups=mesh['col_0'=4,'col_1'=2,'row_0'=4,'row_1'=4] {'col_0','col_1','row_0'}, dimensions={0} | all-to-all | bytes 262144 | tf_op jit(solution)/shard_map/all_to_all | solution.py:44
  663.9 10.1 %all-to-all-done.12 = f32[4,32,1024]{2,1,0:T(8,128)S(1)} async-done(((f32[4,32,1024]{2,1,0:T(8,128)}), f32[4,32,1024]{2,1,0:T(8,128)S(1)}, u32[]{:S(2)}, u32[]{:S(2)}) %all-to-all-start.12) | async-done | bytes 524320 | tf_op jit(solution)/shard_map/all_to_all | solution.py:44
  674.6 11.7 %cholesky.248 = f32[128,128]{1,0:T(8,128)S(1)} custom-call(f32[128,128]{1,0:T(8,128)S(1)} %cholesky.349), custom_call_target="Cholesky" | custom-call | tf_op jit(solution)/shard_map/jit(cholesky)/cholesky | solution.py:90
  686.4 9.8 %custom-call.19 = f32[1,128,128]{1,2,0:T(8,128)S(1)} custom-call(f32[1,128,128]{2,1,0:T(8,128)S(1)} %get-tuple-element.87), custom_call_target="InvertDiagBlocksLowerTriangular" | custom-call | tf_op jit(solution)/shard_map/jit(cholesky)/cholesky | solution.py:90
  696.7 11.7 %cholesky.265 = f32[128,128]{1,0:T(8,128)S(1)} custom-call(f32[128,128]{1,0:T(8,128)S(1)} %convolution_subtract_fusion.6), custom_call_target="Cholesky" | custom-call | tf_op jit(solution)/shard_map/jit(cholesky)/cholesky | solution.py:90
  715.1 19.8 %custom-call.20 = f32[2,128,128]{1,2,0:T(8,128)S(1)} custom-call(f32[2,128,128]{2,1,0:T(8,128)S(1)} %get-tuple-element.31), custom_call_target="InvertDiagBlocksLowerTriangular" | custom-call | tf_op jit(solution)/shard_map/jit(_solve_triangular)/triangular_solve | solution.py:91
  737.9 11.7 %cholesky.282 = f32[128,128]{1,0:T(8,128)S(1)} custom-call(f32[128,128]{1,0:T(8,128)S(1)} %cholesky.352), custom_call_target="Cholesky" | custom-call | tf_op jit(solution)/shard_map/jit(cholesky)/cholesky | solution.py:90
  749.7 9.8 %custom-call.21 = f32[1,128,128]{1,2,0:T(8,128)S(1)} custom-call(f32[1,128,128]{2,1,0:T(8,128)S(1)} %get-tuple-element.83), custom_call_target="InvertDiagBlocksLowerTriangular" | custom-call | tf_op jit(solution)/shard_map/jit(cholesky)/cholesky | solution.py:90
  760.0 11.9 %cholesky.299 = f32[128,128]{1,0:T(8,128)S(1)} custom-call(f32[128,128]{1,0:T(8,128)S(1)} %convolution_subtract_fusion.5), custom_call_target="Cholesky" | custom-call | tf_op jit(solution)/shard_map/jit(cholesky)/cholesky | solution.py:90
  778.6 19.7 %custom-call.22 = f32[2,128,128]{1,2,0:T(8,128)S(1)} custom-call(f32[2,128,128]{2,1,0:T(8,128)S(1)} %get-tuple-element.32), custom_call_target="InvertDiagBlocksLowerTriangular" | custom-call | tf_op jit(solution)/shard_map/jit(_solve_triangular)/triangular_solve | solution.py:91
  801.3 9.1 all_to_all.102
  810.5 10.5 %all_to_all.103 = f32[32,2,256]{2,1,0:T(2,128)S(1)} all-to-all(f32[32,2,256]{2,1,0:T(2,128)S(1)} %reduce_sum.118), channel_id=1, replica_groups=mesh['col_0'=4,'col_1'=2,'row_0'=4,'row_1'=4] {'col_0','col_1','row_0'}, dimensions={0} | all-to-all | bytes 131072 | tf_op jit(solution)/shard_map/all_to_all | solution.py:31
  821.1 11.0 %all_to_all.96 = f32[32,2,256]{2,1,0:T(2,128)S(1)} all-to-all(f32[32,2,256]{2,1,0:T(2,128)S(1)} %broadcast_in_dim.32), channel_id=1, replica_groups=mesh['col_0'=4,'col_1'=2,'row_0'=4,'row_1'=4] {'col_0','col_1','row_0'}, dimensions={0} | all-to-all | bytes 131072 | tf_op jit(solution)/shard_map/all_to_all | solution.py:44
  837.6 6.0 all-to-all-done.16
  844.1 11.7 %cholesky.316 = f32[128,128]{1,0:T(8,128)S(1)} custom-call(f32[128,128]{1,0:T(8,128)S(1)} %cholesky.355), custom_call_target="Cholesky" | custom-call | tf_op jit(solution)/shard_map/jit(cholesky)/cholesky | solution.py:90
  855.8 9.8 %custom-call.23 = f32[1,128,128]{1,2,0:T(8,128)S(1)} custom-call(f32[1,128,128]{2,1,0:T(8,128)S(1)} %get-tuple-element.79), custom_call_target="InvertDiagBlocksLowerTriangular" | custom-call | tf_op jit(solution)/shard_map/jit(cholesky)/cholesky | solution.py:90
  866.1 11.7 %cholesky.333 = f32[128,128]{1,0:T(8,128)S(1)} custom-call(f32[128,128]{1,0:T(8,128)S(1)} %convolution_subtract_fusion.4), custom_call_target="Cholesky" | custom-call | tf_op jit(solution)/shard_map/jit(cholesky)/cholesky | solution.py:90
  884.8 20.0 %custom-call.24 = f32[2,128,128]{1,2,0:T(8,128)S(1)} custom-call(f32[2,128,128]{2,1,0:T(8,128)S(1)} %get-tuple-element.33), custom_call_target="InvertDiagBlocksLowerTriangular" | custom-call | tf_op jit(solution)/shard_map/jit(_solve_triangular)/triangular_solve | solution.py:91
  (173 shorter events, 106.5 us)
Async XLA Ops:
  7.8 165.0 %copy-start.2 = (f32[120]{0:T(128)}, f32[120]{0:T(128)S(1)}, u32[]{:S(2)}) copy-start(f32[120]{0:T(128)S(1)} %compare_convert_fusion) | copy-start | bytes 1444
  12.6 10.8 %all-to-all-start = ((f32[8,5,128]{2,1,0:T(8,128)}), f32[8,5,128]{2,1,0:T(8,128)S(1)}, u32[]{:S(2)}, u32[]{:S(2)}) async-start(f32[8,5,128]{2,1,0:T(8,128)} %fusion.51), calls=%async_computation | async-start | bytes 65536 | tf_op jit(solution)/shard_map/all_to_all | solution.py:23
  18.0 87.5 %all-gather.3.cloned.1.call-start = ((), (), s32[]{:S(2)}) async-start(), calls=%async_computation.17 | async-start | bytes 11141120 | tf_op jit(solution)/shard_map/all_gather | solution.py:123
  154.9 17.9 %copy-start.1 = (s32[120]{0:T(128)S(1)}, s32[120]{0:T(128)}, u32[]{:S(2)}) copy-start(s32[120]{0:T(128)} %param.9) | copy-start | bytes 1444
  205.8 68.0 %copy-start = (f32[640,256]{1,0:T(8,128)S(1)}, f32[640,256]{1,0:T(8,128)}, u32[]{:S(2)}) copy-start(f32[640,256]{1,0:T(8,128)} %param.12) | copy-start | bytes 1966084
  298.0 11.3 %all-to-all-start.5 = ((f32[32,2,256]{2,1,0:T(2,128)}), f32[32,2,256]{2,1,0:T(2,128)S(1)}, u32[]{:S(2)}, u32[]{:S(2)}) async-start(f32[32,2,256]{2,1,0:T(2,128)} %broadcast_in_dim.28), calls=%async_computation.5 | async-start | bytes 131072 | tf_op jit(solution)/shard_map/all_to_all | solution.py:44
  310.1 10.6 %all-to-all-start.6 = ((f32[4,32,2,256]{3,2,1,0:T(2,128)}), f32[4,32,2,256]{3,2,1,0:T(2,128)S(1)}, u32[]{:S(2)}, u32[]{:S(2)}) async-start(f32[4,32,2,256]{3,2,1,0:T(2,128)} %broadcast_in_dim.29), calls=%async_computation.6 | async-start | bytes 524288 | tf_op jit(solution)/shard_map/all_to_all | solution.py:44
  313.5 146.8 %all-gather.5.cloned.1.call-start = ((), (), s32[]{:S(2)}) async-start(), calls=%async_computation.18 | async-start | bytes 11141120 | tf_op jit(solution)/shard_map/all_gather | solution.py:123
  361.7 0.6 copy-start.4
  509.7 17.9 %copy-start.3 = (f32[120]{0:T(128)S(1)}, f32[120]{0:T(128)}, u32[]{:S(2)}) copy-start(f32[120]{0:T(128)} %copy-done.2) | copy-start | bytes 1444
  564.1 54.3 %all-to-all-start.8 = ((f32[4,5,32768]{2,1,0:T(8,128)}), f32[4,5,32768]{2,1,0:T(8,128)}, u32[]{:S(2)}, u32[]{:S(2)}) async-start(f32[4,5,32768]{2,1,0:T(8,128)} %copy.111), calls=%async_computation.8 | async-start | bytes 8388608 | tf_op jit(solution)/shard_map/all_to_all | solution.py:31
  570.3 140.7 %copy-start.5 = (s32[2,2]{1,0:T(2,128)S(1)}, s32[2,2]{1,0:T(2,128)}, u32[]{:S(2)}) copy-start(s32[2,2]{1,0:T(2,128)} %copy-done.4) | copy-start | bytes 52
  660.5 13.6 %all-to-all-start.12 = ((f32[4,32,1024]{2,1,0:T(8,128)}), f32[4,32,1024]{2,1,0:T(8,128)S(1)}, u32[]{:S(2)}, u32[]{:S(2)}) async-start(f32[4,32,1024]{2,1,0:T(8,128)} %broadcast_in_dim.31), calls=%async_computation.12 | async-start | bytes 1048576 | tf_op jit(solution)/shard_map/all_to_all | solution.py:44
  832.8 10.8 %all-to-all-start.16 = ((f32[4,32,2,256]{3,2,1,0:T(2,128)}), f32[4,32,2,256]{3,2,1,0:T(2,128)S(1)}, u32[]{:S(2)}, u32[]{:S(2)}) async-start(f32[4,32,2,256]{3,2,1,0:T(2,128)} %broadcast_in_dim.33), calls=%async_computation.16 | async-start | bytes 524288 | tf_op jit(solution)/shard_map/all_to_all | solution.py:44
Sparse Core Ops, SparseCore 0:
  25.7 79.7 all-gather.2
  384.5 75.7 all-gather.4
where the time goes:
time: 925 us; the launch traced here: 915 us
  other arithmetic  240 us (26%)
  waiting for transfers between devices  239 us (26%)
  blocking collectives  170 us (18%)
  local copies, waits for them, and re-layouts  130 us (14%)
  matrix products  89.4 us (10%)
  starting transfers between devices  24.7 us (3%)
  between operations  21.3 us (2%)
    all_gather x2, waiting for transfers between devices, body(): gathered = lax.all_gather(mapped_scaled, ROW, axis=0, tiled=True)  155 us
    another operation x27, other arithmetic, inverse_lower(): lower = jnp.linalg.cholesky(gram)  138 us
    all_to_all x4, blocking collectives, sum_in_two_steps(): lax.all_to_all(nearer, far, split_axis=0, concat_axis=0, tiled=True)  96.7 us
    another operation x9, other arithmetic, inverse_lower(): jax.scipy.linalg.solve_triangular(lower, jnp.eye(gram.shape[0], dtype=jnp...  79.3 us
    all_to_all x5, blocking collectives, sent_and_summed(): lax.all_to_all(parts, axis, split_axis=0, concat_axis=0, tiled=True)  50.9 us
    all_to_all x1, waiting for transfers between devices, sum_in_two_steps(): lax.all_to_all(nearer, far, split_axis=0, concat_axis=0, tiled=True)  47.9 us
    dot_general x2, matrix products, body(): jnp.einsum('sij,sjk->sik', squares, picked, precision=highest, preferred_...  40.3 us
    reshape x2, local copies, waits for them, and re-layouts, body(): products.reshape(slot_count, tile_size * vec_count)  35.7 us
  transfers between devices with their start and end apart: 8, of which 8 were waited for; matrix products, arithmetic and copies ran while one was open for 0% of the time, Pallas kernels for 0%

commit v1 on v0

v1 whole, which is shorter than its diff:
```python
import functools

import jax
import jax.numpy as jnp
from jax import lax
from jax.experimental import pallas as pl
from jax.experimental.pallas import tpu as pltpu
from jax.sharding import Mesh
from jax.sharding import PartitionSpec as P

Z, K, X, Y = "z", "k", "x", "y"
COL_ROW = (Z, K, X, Y)
ITERS = 2
TILE = 128
VECS = 256
OWN = 5
ROWS = OWN * TILE
GROUPS = 16
DESTS = 8
SLOTS = 120
HALF = 128
ROUTE = ROWS // 2
SUB = ROUTE // 2
BLOCK = 32
HIGHEST = lax.Precision.HIGHEST
MESH = pl.DeviceIdType.MESH
F32 = jnp.float32


def matmul(a, b, contract=((1,), (0,))):
    return lax.dot_general(
        a, b, (contract, ((), ())), precision=HIGHEST, preferred_element_type=F32
    )


def block_inverse(block):
    rows = lax.broadcasted_iota(jnp.int32, (BLOCK, 128), 0)
    lanes = lax.broadcasted_iota(jnp.int32, (BLOCK, 128), 1)
    e = jnp.where(lanes < BLOCK, block, jnp.where(lanes - BLOCK == rows, 1.0, 0.0))
    pivots = jnp.ones((BLOCK, 128), F32)
    for panel in range(BLOCK // 8):
        cols = [
            jnp.broadcast_to(e[:, 8 * panel + j : 8 * panel + j + 1], (BLOCK, 128))
            for j in range(8)
        ]
        for j in range(8):
            k = 8 * panel + j
            d = cols[j][k : k + 1, :]
            pivots = jnp.where(rows == k, d, pivots)
            f = jnp.where(rows > k, cols[j] * (1.0 / d), 0.0)
            for i in range(j + 1, 8):
                cols[i] = cols[i] - f * cols[i][k : k + 1, :]
            e = e - f * e[k : k + 1, :]
    return e * lax.rsqrt(pivots)


def inverse_factor(gram, aug):
    aug[:, 0:VECS] = gram
    r = lax.broadcasted_iota(jnp.int32, (VECS, VECS), 0)
    c = lax.broadcasted_iota(jnp.int32, (VECS, VECS), 1)
    aug[:, VECS:] = jnp.where(r == c, 1.0, 0.0)
    for k0 in range(0, VECS, BLOCK):
        lo = k0 // 128 * 128
        hi = VECS + (k0 + BLOCK + 127) // 128 * 128
        block = aug[k0 : k0 + BLOCK, lo : lo + 128]
        if k0 > lo:
            block = pltpu.roll(block, 128 - (k0 - lo), 1)
        inverse = block_inverse(block)[:, BLOCK : 2 * BLOCK]
        panel = matmul(inverse, aug[k0 : k0 + BLOCK, lo:hi])
        aug[k0 : k0 + BLOCK, lo:hi] = panel
        if k0 + BLOCK < VECS:
            below = panel[:, : VECS - lo].T[k0 + BLOCK - lo :, :]
            aug[k0 + BLOCK :, lo:hi] = aug[k0 + BLOCK :, lo:hi] - matmul(below, panel)
    return aug[:, VECS:]


def place(axis, offset):
    return lax.rem(lax.axis_index(axis) + (offset + 4), 4)


class Sems:
    def __init__(self, send, recv):
        self.send, self.recv, self.used = send, recv, 0

    def copy(self, src, dst, device):
        i = self.used
        self.used += 1
        return pltpu.make_async_remote_copy(
            src_ref=src,
            dst_ref=dst,
            send_sem=self.send.at[i],
            recv_sem=self.recv.at[i],
            device_id=device,
            device_id_type=MESH,
        )


class Gather:
    def __init__(self, field, sems):
        self.field, self.sems, self.all = field, sems, []
        self.p1, self.q, self.f1, self.f2 = {}, {}, {}, {}

    def slot(self, route, d1, d2):
        dx, dy = (d1, d2) if route == 0 else (d2, d1)
        return place(X, dx) * 4 + place(Y, dy)

    def send(self, route, slot, start, size, along, sign):
        axis = (X, Y)[route ^ along]
        part = self.field.at[slot, pl.ds(route * ROUTE + start, size)]
        c = self.sems.copy(part, part, {axis: place(axis, sign)})
        c.start()
        self.all.append(c)
        return c

    def begin(self):
        for route in (0, 1):
            for s in (1, -1):
                self.p1[route, s] = self.send(route, self.slot(route, 0, 0), 0, ROUTE, 0, s)
        for route in (0, 1):
            self.spread(route, 0)

    def spread(self, route, d1):
        for s in (1, -1):
            self.q[route, d1, s] = self.send(route, self.slot(route, d1, 0), 0, ROUTE, 1, s)

    def sub(self, sign):
        return 0 if sign > 0 else SUB

    def near(self):
        for route in (0, 1):
            for s in (1, -1):
                self.p1[route, s].wait_recv()
                self.f1[route, s] = self.send(
                    route, self.slot(route, -s, 0), self.sub(s), SUB, 0, s
                )
        for route in (0, 1):
            for s in (1, -1):
                self.spread(route, -s)

    def far(self):
        for route in (0, 1):
            for s in (1, -1):
                self.f1[route, s].wait_recv()
            self.spread(route, 2)

    def onward(self, which):
        for d1 in which:
            for route in (0, 1):
                for s in (1, -1):
                    self.q[route, d1, s].wait_recv()
                    self.f2[route, d1, s] = self.send(
                        route, self.slot(route, d1, -s), self.sub(s), SUB, 1, s
                    )

    def finish(self):
        for c in self.f2.values():
            c.wait_recv()

    def sent(self):
        for c in self.all:
            c.wait_send()


class Scatter:
    def __init__(self, terms, pair, arrived, sems):
        self.terms, self.pair, self.arrived, self.sems = terms, pair, arrived, sems
        self.all, self.first, self.direct, self.last = [], {}, {}, {}

    def go(self, src, dst, device):
        c = self.sems.copy(src, dst, device)
        c.start()
        self.all.append(c)
        return c

    def begin(self):
        other = 1 - lax.axis_index(K)
        for d in (2, 1, -1, 0):
            self.first[d] = self.go(
                self.terms.at[other, place(Z, d)], self.pair.at[d % 4], {K: other}
            )

    def combine(self, d):
        self.first[d].wait_recv()
        mine = lax.axis_index(K)
        self.pair[d % 4] = self.pair[d % 4] + self.terms[mine, place(Z, d)]

    def rows(self, part):
        return pl.ds(part * ROUTE, ROUTE)

    def ring(self):
        self.combine(2)
        for part, s in ((0, 1), (1, -1)):
            self.direct[2, s] = self.go(
                self.pair.at[2, self.rows(part)], self.arrived.at[part], {Z: place(Z, s)}
            )
        for part, s in ((1, 1), (0, -1)):
            self.combine(s)
            self.direct[1, s] = self.go(
                self.pair.at[s % 4, self.rows(part)], self.arrived.at[2 + part], {Z: place(Z, s)}
            )
        for part, s in ((0, 1), (1, -1)):
            self.direct[2, s].wait_recv()
            self.pair[s % 4, self.rows(part)] = (
                self.pair[s % 4, self.rows(part)] + self.arrived[part]
            )
            self.last[s] = self.go(
                self.pair.at[s % 4, self.rows(part)], self.arrived.at[4 + part], {Z: place(Z, s)}
            )
        self.combine(0)

    def total(self, put):
        for s in (1, -1):
            self.direct[1, s].wait_recv()
            self.last[s].wait_recv()
        for part in (0, 1):
            put(
                part,
                self.pair[0, self.rows(part)] + self.arrived[2 + part] + self.arrived[4 + part],
            )

    def sent(self):
        for c in self.all:
            c.wait_send()


class GramSum:
    def __init__(self, own, parts, piece, pieces, whole, sems):
        self.own, self.parts, self.piece, self.pieces, self.whole = own, parts, piece, pieces, whole
        self.sems, self.all = sems, []

    def go(self, src, dst, device):
        c = self.sems.copy(src, dst, device)
        c.start()
        self.all.append(c)
        return c

    def peers(self):
        for dx in range(4):
            for dy in range(4):
                if dx or dy:
                    yield place(X, dx), place(Y, dy)

    def begin(self):
        me = lax.axis_index(X) * 4 + lax.axis_index(Y)
        self.one = [
            self.go(self.own.at[x * 4 + y], self.parts.at[me], {X: x, Y: y})
            for x, y in self.peers()
        ]
        self.parts[me] = self.own[me]

    def across(self):
        for c in self.one:
            c.wait_recv()
        total = self.parts[0]
        for i in range(1, GROUPS):
            total = total + self.parts[i]
        self.piece[...] = total
        z, k = lax.axis_index(Z), lax.axis_index(K)
        me = z * 2 + k
        self.two = []
        for dk in range(2):
            for dz in range(4):
                if dk or dz:
                    to = {Z: place(Z, dz), K: lax.rem(k + dk, 2)}
                    self.two.append(self.go(self.piece, self.pieces.at[me], to))
        self.pieces[me] = total

    def back(self):
        for c in self.two:
            c.wait_recv()
        total = self.pieces[0]
        for i in range(1, DESTS):
            total = total + self.pieces[i]
        me = lax.axis_index(X) * 4 + lax.axis_index(Y)
        self.whole[me] = total
        self.three = [
            self.go(self.whole.at[me], self.whole.at[me], {X: x, Y: y}) for x, y in self.peers()
        ]

    def result(self):
        for c in self.three:
            c.wait_recv()
        return self.whole[...].reshape(VECS, VECS)

    def sent(self):
        for c in self.all:
            c.wait_send()


GRAM_COPIES = 15 + 7 + 15
GATHER_COPIES = 40
SCATTER_COPIES = 10


def gram_scratch():
    return [
        pltpu.VMEM((GROUPS, 16, VECS), F32),
        pltpu.VMEM((GROUPS, 16, VECS), F32),
        pltpu.VMEM((16, VECS), F32),
        pltpu.VMEM((DESTS, 16, VECS), F32),
        pltpu.VMEM((GROUPS, 16, VECS), F32),
        pltpu.SemaphoreType.DMA((GRAM_COPIES,)),
        pltpu.SemaphoreType.DMA((GRAM_COPIES,)),
    ]


def gram_of(refs):
    return GramSum(*refs[:5], Sems(*refs[5:]))


def split_panels(field, split, scale):
    def group(r, _):
        if scale is not None:
            cols = scale[r].T
        for t in range(OWN):
            v = field[r, pl.ds(t * TILE, TILE), :]
            if scale is not None:
                v = v * cols[:, t : t + 1]
            high = v.astype(jnp.bfloat16)
            split[r * OWN + t, 0:TILE, :] = high
            split[r * OWN + t, TILE:, :] = (v - high.astype(F32)).astype(jnp.bfloat16)
        return 0

    lax.fori_loop(0, GROUPS, group, 0)


UNROLL = 8


def tile_products(tiles, split, order, source, keep, running):
    def step(i, total):
        for j in range(UNROLL):
            s = i * UNROLL + j
            tile = tiles[order[s]]
            both = jnp.concatenate([tile, tile], axis=1)
            y = jnp.dot(both, split[source[s]], preferred_element_type=F32)
            total = y + keep[s] * total
            running[s] = total
        return total

    lax.fori_loop(0, SLOTS // UNROLL, step, jnp.zeros((TILE, HALF), F32))


def tile_terms(running, last, has, terms):
    def dest(c, _):
        z, k = c // 2, lax.rem(c, 2)
        for t in range(OWN):
            i = c * OWN + t
            terms[k, z, pl.ds(t * TILE, TILE), :] = has[i] * running[last[i]]
        return 0

    lax.fori_loop(0, DESTS, dest, 0)


def load_tiles(affinity, tiles, sem):
    c = pltpu.make_async_copy(affinity, tiles, sem)
    c.start()
    return c


def spread_scale(row, scale):
    cols = row[...].T
    for t in range(OWN):
        scale[pl.ds(t * TILE, TILE), :] = jnp.broadcast_to(cols[:, t : t + 1], (TILE, 128))


def half(h):
    return pl.ds(h * HALF, HALF)


def first_kernel(
    order, source, keep, last, has, start, affinity, image, scale,
    tiles, field, split, running, terms, pair, arrived, sums, degree_out, degree_in, scales,
    tile_sem, gather_send, gather_recv, scatter_send, scatter_recv, small_send, small_recv,
):
    tile_copy = load_tiles(affinity, tiles, tile_sem)
    x, y, z, k = (lax.axis_index(a) for a in (X, Y, Z, K))
    me, col = x * 4 + y, z * 2 + k
    gathers = [
        Gather(field.at[h], Sems(gather_send.at[h], gather_recv.at[h])) for h in range(2)
    ]
    scatters = [
        Scatter(terms.at[h], pair.at[h], arrived.at[h], Sems(scatter_send.at[h], scatter_recv.at[h]))
        for h in range(2)
    ]
    small = Sems(small_send, small_recv)
    smalls = []
    for h in range(2):
        field[h, me] = start[:, h * HALF : (h + 1) * HALF]
    gathers[0].begin()
    tile_copy.wait()

    ones = jnp.ones((8, TILE), jnp.bfloat16)

    def row_sums(i, total):
        for j in range(UNROLL):
            s = i * UNROLL + j
            d = lax.dot_general(
                ones, tiles[order[s]], (((1,), (1,)), ((), ())), preferred_element_type=F32
            )
            total = d + keep[s] * total
            sums[s] = total
        return total

    lax.fori_loop(0, SLOTS // UNROLL, row_sums, jnp.zeros((8, TILE), F32))
    for c in range(DESTS):
        for t in range(8):
            i = c * OWN + t
            if t < OWN:
                degree_out[c, t : t + 1, :] = (has[i] * sums[last[i]])[0:1]
            else:
                degree_out[c, t : t + 1, :] = jnp.zeros((1, TILE), F32)
    for dk in range(2):
        for dz in range(4):
            if dk or dz:
                pz, pk = place(Z, dz), lax.rem(k + dk, 2)
                c = small.copy(degree_out.at[pz * 2 + pk], degree_in.at[col], {Z: pz, K: pk})
                c.start()
                smalls.append(c)
    degree_in[col] = degree_out[col]
    gathers[0].near()
    for c in smalls:
        c.wait_recv()
    degree = degree_in[0]
    for c in range(1, DESTS):
        degree = degree + degree_in[c]
    scales[me] = 1.0 / jnp.sqrt(1.0 + degree)
    gathered = []
    for dx in range(4):
        for dy in range(4):
            if dx or dy:
                c = small.copy(
                    scales.at[me], scales.at[me], {X: place(X, dx), Y: place(Y, dy)}
                )
                c.start()
                gathered.append(c)
    spread_scale(scales.at[me], scale)
    gathers[0].far()
    gathers[1].begin()
    gathers[0].onward((0, 1, -1, 2))
    for c in gathered:
        c.wait_recv()
    gathers[1].near()
    gathers[0].finish()

    def products(h):
        split_panels(field.at[h], split, scales)
        tile_products(tiles, split, order, source, keep, running)
        tile_terms(running, last, has, terms.at[h])
        scatters[h].begin()

    products(0)
    gathers[1].far()
    scatters[0].ring()
    gathers[1].onward((0, 1, -1, 2))
    gathers[1].finish()
    products(1)
    scatters[1].ring()

    def put(h, part, total):
        rows = pl.ds(part * ROUTE, ROUTE)
        s = scale[rows]
        image[rows, half(h)] = s * (s * start[rows, half(h)] + total)

    for h in range(2):
        scatters[h].total(functools.partial(put, h))
    for c in smalls + gathered:
        c.wait_send()
    for h in range(2):
        gathers[h].sent()
        scatters[h].sent()


def second_kernel(
    order, source, keep, last, has, image, scale, affinity, vectors, firsts,
    tiles, field, split, running, terms, pair, arrived, aug, work,
    tile_sem, gather_send, gather_recv, scatter_send, scatter_recv, *gram_refs,
):
    tile_copy = load_tiles(affinity, tiles, tile_sem)
    x, y = (lax.axis_index(a) for a in (X, Y))
    me = x * 4 + y
    gathers = [
        Gather(field.at[h], Sems(gather_send.at[h], gather_recv.at[h])) for h in range(2)
    ]
    scatters = [
        Scatter(terms.at[h], pair.at[h], arrived.at[h], Sems(scatter_send.at[h], scatter_recv.at[h]))
        for h in range(2)
    ]
    grams = [gram_of(gram_refs[7 * i : 7 * i + 7]) for i in range(4)]
    root = jnp.sqrt(F32(ROWS * GROUPS * DESTS))

    def local_gram(g, matrix):
        grams[g].own[...] = matmul(matrix, matrix, ((0,), (0,))).reshape(GROUPS, 16, VECS)
        grams[g].begin()

    for h in range(2):
        field[h, me] = scale[...] * image[:, half(h)]
    gathers[0].begin()
    local_gram(0, image[...])
    gathers[0].near()
    grams[0].across()
    gathers[0].far()
    gathers[1].begin()
    grams[0].back()
    inverse_one = inverse_factor(grams[0].result(), aug)
    gathers[0].onward((0, 1, -1, 2))
    first = matmul(image[...], inverse_one, ((1,), (1,)))
    firsts[0] = root * first
    work[0] = inverse_one
    local_gram(1, first)
    gathers[1].near()
    grams[1].across()
    tile_copy.wait()

    def products(h):
        split_panels(field.at[h], split, None)
        tile_products(tiles, split, order, source, keep, running)
        tile_terms(running, last, has, terms.at[h])
        scatters[h].begin()

    gathers[0].finish()
    gathers[1].far()
    grams[1].back()
    products(0)
    gathers[1].onward((0, 1, -1, 2))
    scatters[0].ring()
    gathers[1].finish()
    products(1)
    scatters[1].ring()
    inverse_two = inverse_factor(grams[1].result(), aug)
    both = matmul(inverse_two, work[0])

    def put(h, part, total):
        rows = pl.ds(part * ROUTE, ROUTE)
        s = scale[rows]
        vectors[rows, half(h)] = s * (s * image[rows, half(h)] + total)

    for h in range(2):
        scatters[h].total(functools.partial(put, h))
    mapped = matmul(vectors[...], both, ((1,), (1,)))
    local_gram(2, mapped)
    grams[2].across()
    grams[2].back()
    first = matmul(mapped, inverse_factor(grams[2].result(), aug), ((1,), (1,)))
    local_gram(3, first)
    firsts[1] = root * first
    grams[3].across()
    grams[3].back()
    vectors[...] = root * matmul(first, inverse_factor(grams[3].result(), aug), ((1,), (1,)))
    for h in range(2):
        gathers[h].sent()
        scatters[h].sent()
    for g in grams:
        g.sent()


def sweep_scratch():
    return [
        pltpu.VMEM((SLOTS, TILE, TILE), jnp.bfloat16),
        pltpu.VMEM((2, GROUPS, ROWS, HALF), F32),
        pltpu.VMEM((GROUPS * OWN, 2 * TILE, HALF), jnp.bfloat16),
        pltpu.VMEM((SLOTS, TILE, HALF), F32),
        pltpu.VMEM((2, 2, 4, ROWS, HALF), F32),
        pltpu.VMEM((2, 4, ROWS, HALF), F32),
        pltpu.VMEM((2, 6, ROUTE, HALF), F32),
    ]


def sweep_semaphores():
    return [
        pltpu.SemaphoreType.DMA,
        pltpu.SemaphoreType.DMA((2, GATHER_COPIES)),
        pltpu.SemaphoreType.DMA((2, GATHER_COPIES)),
        pltpu.SemaphoreType.DMA((2, SCATTER_COPIES)),
        pltpu.SemaphoreType.DMA((2, SCATTER_COPIES)),
    ]


def slot_order(tile_rows, tile_cols, live_tiles):
    slot = jnp.arange(SLOTS)
    key = jnp.where(slot < live_tiles[0], tile_rows, DESTS * OWN)
    before = (key[None, :] < key[:, None]) | (
        (key[None, :] == key[:, None]) & (slot[None, :] < slot[:, None])
    )
    rank = jnp.sum(before.astype(jnp.int32), axis=1)
    at = rank[None, :] == slot[:, None]
    order = jnp.sum(jnp.where(at, slot[None, :], 0), axis=1)
    source = jnp.sum(jnp.where(at, tile_cols[None, :], 0), axis=1)
    follows = (rank[None, :] == slot[:, None] - 1).astype(jnp.int32)
    keys = jnp.sum(jnp.where(at, key[None, :], 0), axis=1)
    previous = jnp.sum(follows * (key[None, :] + 1), axis=1) - 1
    keep = (keys == previous).astype(F32)
    row = jnp.arange(DESTS * OWN)
    last = jnp.maximum(jnp.sum((key[None, :] <= row[:, None]).astype(jnp.int32), axis=1) - 1, 0)
    has = jnp.any(key[None, :] == row[:, None], axis=1).astype(F32)
    return order.astype(jnp.int32), source.astype(jnp.int32), keep, last, has


def body(affinity, tile_rows, tile_cols, live_tiles, start):
    slots = slot_order(tile_rows, tile_cols, live_tiles)
    smem = pl.BlockSpec(memory_space=pltpu.SMEM)
    vmem = pl.BlockSpec(memory_space=pltpu.VMEM)
    anywhere = pl.BlockSpec(memory_space=pl.ANY)
    params = pltpu.CompilerParams(has_side_effects=True, vmem_limit_bytes=56 << 20)
    image, scale = pl.pallas_call(
        first_kernel,
        out_shape=(
            jax.ShapeDtypeStruct((ROWS, VECS), F32),
            jax.ShapeDtypeStruct((ROWS, HALF), F32),
        ),
        in_specs=[smem] * 5 + [vmem, anywhere],
        out_specs=(vmem, vmem),
        scratch_shapes=sweep_scratch()
        + [
            pltpu.VMEM((SLOTS, 8, TILE), F32),
            pltpu.VMEM((DESTS, 8, TILE), F32),
            pltpu.VMEM((DESTS, 8, TILE), F32),
            pltpu.VMEM((GROUPS, 8, TILE), F32),
        ]
        + sweep_semaphores()
        + [pltpu.SemaphoreType.DMA((22,)), pltpu.SemaphoreType.DMA((22,))],
        compiler_params=params,
        name="first_sweep",
    )(*slots, start, affinity)
    vectors, firsts = pl.pallas_call(
        second_kernel,
        out_shape=(
            jax.ShapeDtypeStruct((ROWS, VECS), F32),
            jax.ShapeDtypeStruct((ITERS, ROWS, VECS), F32),
        ),
        in_specs=[smem] * 5 + [vmem, vmem, anywhere],
        out_specs=(vmem, vmem),
        scratch_shapes=sweep_scratch()
        + [pltpu.VMEM((VECS, 2 * VECS), F32), pltpu.VMEM((1, VECS, VECS), F32)]
        + sweep_semaphores()
        + gram_scratch() * 4,
        compiler_params=params,
        name="second_sweep",
    )(*slots, image, scale, affinity)
    return vectors, firsts


def solution(mesh):
    torus = Mesh(mesh.devices.reshape(4, 2, 4, 4), COL_ROW)
    return jax.shard_map(
        body,
        mesh=torus,
        in_specs=(P(COL_ROW, None, None), P(COL_ROW), P(COL_ROW), P(COL_ROW), P(COL_ROW, None)),
        out_specs=(P(COL_ROW, None), P(None, COL_ROW, None)),
        check_vma=False,
    )
```

time: 925 us -> 299 us (0.32)
  Pallas kernels: 0 us -> 287 us
  waiting for transfers between devices: 239 us -> 0 us
  other arithmetic: 240 us -> 4.01 us
  blocking collectives: 170 us -> 0 us
  local copies, waits for them, and re-layouts: 130 us -> 3.13 us
  matrix products: 89.4 us -> 0 us
  starting transfers between devices: 24.7 us -> 0 us
  between operations: 21.3 us -> 1.54 us
    pallas_call x0 -> x2, Pallas kernels: none -> 287 us  [the longest x1 184 us: body(): pl.pallas_call(second_kernel, out_shape=(jax.ShapeDtypeStruct((ROWS, VECS...]
    another operation x36 -> x0, other arithmetic: 217 us -> none  [the longest x27 138 us: inverse_lower(): lower = jnp.linalg.cholesky(gram)]
    all_to_all x11 -> x0, blocking collectives: 170 us -> none  [the longest x4 96.7 us: sum_in_two_steps(): lax.all_to_all(nearer, far, split_axis=0, concat_axis=0, tiled=True)]
    all_gather x2 -> x0, waiting for transfers between devices: 155 us -> none  [body(): gathered = lax.all_gather(mapped_scaled, ROW, axis=0, tiled=True)]
    dot_general x15 -> x0, matrix products: 84 us -> none  [the longest x2 40.3 us: body(): jnp.einsum('sij,sjk->sik', squares, picked, precision=highest, preferred_...]
    all_to_all x6 -> x0, waiting for transfers between devices: 83.9 us -> none  [the longest x1 47.9 us: sum_in_two_steps(): lax.all_to_all(nearer, far, split_axis=0, concat_axis=0, tiled=True)]
    reshape x7 -> x0, local copies, waits for them, and re-layouts: 36.8 us -> none  [the longest x2 35.7 us: body(): products.reshape(slot_count, tile_size * vec_count)]
    dot_general x3 -> x0, local copies, waits for them, and re-layouts: 31.4 us -> none  [the longest x2 31.2 us: body(): jnp.einsum('sij,sjk->sik', squares, picked, precision=highest, preferred_...]
  transfers between devices with their start and end apart: 8 -> 0, of which waited for: 8 -> 0; matrix products, arithmetic and copies ran while one was open for 0% -> 0% of each run, Pallas kernels for 0% -> 0%
where the time goes in v1:
time: 299 us; the launch traced here: 296 us
  Pallas kernels  287 us (96%)
  other arithmetic  4.01 us (1%)
  local copies, waits for them, and re-layouts  3.13 us (1%)
    pallas_call x1, Pallas kernels, body(): pl.pallas_call(second_kernel, out_shape=(jax.ShapeDtypeStruct((ROWS, VECS...  184 us
    pallas_call x1, Pallas kernels, body(): pl.pallas_call(first_kernel, out_shape=(jax.ShapeDtypeStruct((ROWS, VECS)...  103 us

profile of v1, /device:TPU:0, one launch (start us, length us, event | category | flops | bytes accessed | tf_op | source)
XLA Modules:
  0.0 295.7 jit_solution(15833389428103760088)
XLA Ops:
  1.3 0.7 broadcast_add_fusion
  1.9 0.1 convert_reduce_fusion.1
  2.0 0.6 add_maximum_fusion.last
  2.6 0.1 fusion.2
  2.7 0.5 convert_element_type.16.has
  3.2 0.2 convert_reduce_fusion
  3.4 1.4 select_reduce_fusion
  4.8 0.5 compare_convert_fusion.keep
  5.3 103.2 %first_sweep.1 = (f32[640,256]{1,0:T(8,128)}, f32[640,128]{1,0:T(8,128)}) custom-call(s32[120]{0:T(128)} %get-tuple-element.9.order, s32[120]{0:T(128)} %get-tuple-element.8.source, f32[120]{0:T(128)} %compare_convert_fusion.keep, s32[40]{0:T(128)} %add_maximum_fusion.last, f32[40]{0:T(128)} %convert_element_type.16.has, f32[640,256]{1,0:T(8,128)} %start.1, ...), custom_call_target="tpu_custom_call" | custom-call | tf_op jit(solution)/shard_map/first_sweep/pallas_call | solution.py:605
  108.6 183.8 %second_sweep.1 = (f32[640,256]{1,0:T(8,128)}, f32[2,640,256]{2,1,0:T(8,128)}) custom-call(s32[120]{0:T(128)} %get-tuple-element.9.order, s32[120]{0:T(128)} %get-tuple-element.8.source, f32[120]{0:T(128)} %compare_convert_fusion.keep, s32[40]{0:T(128)} %add_maximum_fusion.last, f32[40]{0:T(128)} %convert_element_type.16.has, ...), custom_call_target="tpu_custom_call" | custom-call | tf_op jit(solution)/shard_map/second_sweep/pallas_call | solution.py:625
  292.3 0.0 copy-start
  292.3 2.1 copy.10
  294.4 0.0 copy-done
  294.4 1.1 copy.11
Async XLA Ops:
  292.3 2.1 copy-start
